TPU v7x, 128 devices: a whole 4x4x4 slice. The times are simulated.
128 devices in a mesh: req: 16 (over y, z_lo, core), ctx: 8 (over z_hi, x).
Axes of the slice: x: 4, y: 4, z: 4 (z_hi: 2, z_lo: 2; z = z_hi * 2 + z_lo), core: 2. Of those that a mesh axis runs over, the one named last changes fastest.
Arguments:
- queries: bfloat16 [16, 1024, 64, 128], P('req', 'ctx'), may hold values from -6 to 6
- span_keys: bfloat16 [16, 1024, 4, 128], P('req', 'ctx'), may hold values from -6 to 6
- span_values: bfloat16 [16, 1024, 4, 128], P('req', 'ctx'), may hold values from -6 to 6
- store_keys: bfloat16 [8, 512, 32, 4, 128], P('ctx', 'req'), may hold values from -6 to 6
- store_values: bfloat16 [8, 512, 32, 4, 128], P('ctx', 'req'), may hold values from -6 to 6
- page_home: int32 [8, 512], P('ctx'), may hold values from 0 to 511, as said below
- hits: int32 [16, 128], replicated, may hold values from 0 to 511, as said below
- counts: int32 [16], replicated, may hold values from 1 to 128, as said below
Outputs:
- attended: bfloat16 [16, 1024, 64, 128], P('req', 'ctx')
Inputs may be any that keep to these rules, and one draw needn't show every extreme that they name: page_home[c] is a permutation of the storage rows 0 to 511 for each cycle slot c; storage row s of slot c lies on the store device of req index s // 32 and ctx index c. `hits`: entries j >= counts[r] are padding; for each request and each cycle slot c, of the 16 entries j with j mod 8 = c (padding included) exactly 1 lie on each req index of the store. `counts`: some request has exactly 128 cached pages.
All inputs are finite; a program needn't handle non-finite values.
Results may differ from a plain program's by a relative error of at most 0.0065.
Values may be sent and summed in bfloat16 or wider, within the bound.
A program may use at most 384 MiB of HBM per device.

v0:
```python
import jax
import jax.numpy as jnp
from jax import lax
from jax.sharding import PartitionSpec as P


def attend(carry, query_groups, keys, values, visible):
    peak, total, summed = carry
    scores = jnp.einsum("tkgd,skd->tkgs", query_groups, keys, preferred_element_type=jnp.float32)
    scores = scores * query_groups.shape[-1] ** (-0.5)
    scores = jnp.where(visible[:, None, None, :], scores, -jnp.inf)
    new_peak = jnp.maximum(peak, jnp.max(scores, axis=-1))
    weights = jnp.exp(scores - new_peak[..., None])
    factor = jnp.exp(peak - new_peak)
    total = total * factor + jnp.sum(weights, axis=-1)
    summed = summed * factor[..., None] + jnp.einsum(
        "tkgs,skd->tkgd", weights.astype(jnp.bfloat16), values, preferred_element_type=jnp.float32
    )
    return (new_peak, total, summed)


def per_device(queries, span_keys, span_values, store_keys, store_values, page_home, hits, counts):
    n_req = lax.axis_size("req")
    n_ctx = lax.axis_size("ctx")
    group_index = lax.axis_index("req")
    cycle_index = lax.axis_index("ctx")
    tokens = queries.shape[1]
    heads = queries.shape[2]
    head_size = queries.shape[3]
    kv_heads = span_keys.shape[2]
    page_len = store_keys.shape[2]
    store_dev = store_keys.shape[1]
    store_rows = page_home.shape[1]
    page_dev = hits.shape[1] // n_ctx
    per_src = page_dev // n_req
    sub_rows = 512
    query_groups = queries[0].reshape(tokens, kv_heads, heads // kv_heads, head_size)
    query_pos = cycle_index * tokens + jnp.arange(tokens, dtype=jnp.int32)
    count_here = lax.dynamic_index_in_dim(counts, group_index, 0, keepdims=False)
    slot_hits = hits.reshape(n_req, page_dev, n_ctx)
    page_ids = lax.dynamic_index_in_dim(slot_hits, cycle_index, 2, keepdims=False)
    matches = page_ids[:, :, None] == jnp.arange(store_rows, dtype=jnp.int32)[None, None, :]
    rows = jnp.sum(jnp.where(matches, page_home[0][None, None, :], 0), axis=-1)
    source = rows // store_dev
    page_pos = jnp.arange(page_dev, dtype=jnp.int32)
    earlier = page_pos[None, :] < page_pos[:, None]
    same_source = source[:, :, None] == source[:, None, :]
    rank = jnp.sum((same_source & earlier[None]).astype(jnp.int32), axis=2)
    live = page_pos[None, :] * n_ctx + cycle_index < counts[:, None]
    mine = source == group_index
    select = mine[:, None, :] & (
        rank[:, None, :] == jnp.arange(per_src, dtype=jnp.int32)[None, :, None]
    )
    local_slot = jnp.sum(jnp.where(select, (rows % store_dev)[:, None, :], 0), axis=2)
    send_live = jnp.any(select & live[:, None, :], axis=2)
    keep = send_live[:, :, None, None, None]
    send_keys = jnp.where(keep, store_keys[0][local_slot], jnp.zeros((), jnp.bfloat16))
    send_values = jnp.where(keep, store_values[0][local_slot], jnp.zeros((), jnp.bfloat16))
    start_carry = (
        jnp.full((tokens, kv_heads, heads // kv_heads), -1e30, jnp.float32),
        jnp.zeros((tokens, kv_heads, heads // kv_heads), jnp.float32),
        jnp.zeros((tokens, kv_heads, heads // kv_heads, head_size), jnp.float32),
    )
    received = (
        lax.all_to_all(send_keys, "req", split_axis=0, concat_axis=0, tiled=True),
        lax.all_to_all(send_values, "req", split_axis=0, concat_axis=0, tiled=True),
    )
    flat_keys = received[0].reshape((n_req * per_src, page_len, kv_heads, head_size))
    flat_values = received[1].reshape((n_req * per_src, page_len, kv_heads, head_size))
    source_here = lax.dynamic_index_in_dim(source, group_index, 0, keepdims=False)
    rank_here = lax.dynamic_index_in_dim(rank, group_index, 0, keepdims=False)
    order = source_here * per_src + rank_here
    pages_keys = flat_keys[order].reshape(page_dev * page_len, kv_heads, head_size)
    pages_values = flat_values[order].reshape(page_dev * page_len, kv_heads, head_size)
    block_keys = jnp.concatenate([pages_keys, span_keys[0]], axis=0)
    block_values = jnp.concatenate([pages_values, span_values[0]], axis=0)
    block_rows = page_dev * page_len + tokens
    prefix_rows = page_dev * page_len
    carry = start_carry
    piece = (
        lax.all_gather(block_keys, "ctx", axis=0, tiled=True),
        lax.all_gather(block_values, "ctx", axis=0, tiled=True),
    )
    start = jnp.int32(0)
    total_rows = piece[0].shape[0]
    for offset in range(0, total_rows, sub_rows):
        size = min(sub_rows, total_rows - offset)
        index = start + offset + jnp.arange(size, dtype=jnp.int32)
        owner = index // block_rows
        within = index % block_rows
        is_prefix = within < prefix_rows
        page_live = within // page_len * n_ctx + owner < count_here
        key_pos = owner * tokens + within - prefix_rows
        visible = jnp.where(
            is_prefix[None, :], page_live[None, :], key_pos[None, :] <= query_pos[:, None]
        )
        carry = attend(
            carry,
            query_groups,
            piece[0][offset : offset + size],
            piece[1][offset : offset + size],
            visible,
        )
    peak, total, summed = carry
    result = (summed / total[..., None]).astype(jnp.bfloat16)
    return result.reshape(1, tokens, heads, head_size)


def solution(mesh):
    placed = (
        P("req", "ctx", None, None),
        P("req", "ctx", None, None),
        P("req", "ctx", None, None),
        P("ctx", "req", None, None, None),
        P("ctx", "req", None, None, None),
        P("ctx", None),
        P(),
        P(),
    )
    return jax.shard_map(
        per_device,
        mesh=mesh,
        in_specs=placed,
        out_specs=P("req", "ctx", None, None),
        check_vma=False,
    )
```

profile of v0, /device:TPU:64, one launch (start us, length us, event | category | flops | bytes accessed | tf_op | source)
XLA Modules:
  0.0 414.6 jit_solution(6198489587037423402)
XLA Ops:
  6.5 0.9 copy.151
  7.5 0.1 copy.152
  7.6 1.1 select_reduce_fusion
  8.7 0.4 convert_reduce_fusion
  9.2 0.8 and_reduce_fusion
  10.0 0.1 fusion.86
  10.1 2.4 copy.257
  12.6 1.4 copy.256
  14.0 2.6 gather_fusion
  16.6 1.4 gather_fusion.2
  18.1 2.3 fusion.83
  20.4 5.6 %all-to-all-start = ((bf16[16,1,32,4,128]{4,2,3,1,0:T(8,128)(2,1)}), bf16[16,1,32,4,128]{4,2,3,1,0:T(8,128)(2,1)S(1)}, u32[]{:S(2)}, u32[]{:S(2)}) async-start(bf16[16,1,32,4,128]{4,2,3,1,0:T(8,128)(2,1)} %get-tuple-element.29), calls=%async_computation | async-start | bytes 1048576 | tf_op jit(solution)/shard_map/all_to_all | solution.py:65
  26.0 0.9 copy.258
  27.0 9.8 %all-to-all-done = bf16[16,1,32,4,128]{4,2,3,1,0:T(8,128)(2,1)S(1)} async-done(((bf16[16,1,32,4,128]{4,2,3,1,0:T(8,128)(2,1)}), bf16[16,1,32,4,128]{4,2,3,1,0:T(8,128)(2,1)S(1)}, u32[]{:S(2)}, u32[]{:S(2)}) %all-to-all-start) | async-done | bytes 524320 | tf_op jit(solution)/shard_map/all_to_all | solution.py:65
  36.9 0.6 gather_fusion.1
  37.6 0.9 pad_maximum_fusion
  38.5 3.6 all-to-all-start.1
  42.1 0.6 all-gather.5.cloned.1.call-start
  42.6 1.3 dynamic_slice.15
  44.0 0.7 fusion.91
  44.7 0.7 fusion.151
  45.4 0.7 fusion.153
  46.1 0.7 fusion.155
  46.9 0.7 fusion.149
  47.7 1.7 copy.161
  49.4 2.1 compare_select_fusion.3
  51.5 1.6 compare_select_fusion.9
  53.1 0.6 gather_fusion.3
  53.7 0.9 copy.160
  54.6 1.3 copy.162
  55.8 1.8 pad_maximum_fusion.1
  57.7 57.7 %all-gather.3.cloned.1.call-done = bf16[5120,4,128]{2,0,1:T(8,128)(2,1)} async-done(((bf16[640,4,128]{2,0,1:T(8,128)(2,1)}), bf16[5120,4,128]{2,0,1:T(8,128)(2,1)}) %all-gather.3.cloned.1.call-update) | async-done | bytes 5242896 | tf_op jit(solution)/shard_map/all_gather | solution.py:81
  115.4 10.3 %fusion.25 = (f32[128,4,16]{0,2,1:T(8,128)S(1)}, f32[4,512,128,16]{2,1,3,0:T(8,128)}) fusion(pred[128,512]{0,1:T(8,128)(4,1)S(1)} %get-tuple-element.35, bf16[128,4,16,128]{3,2,1,0:T(8,128)(2,1)S(1)} %bitcast.321, bf16[5120,4,128]{2,0,1:T(8,128)(2,1)} %all-gather.3.cloned.1.call-done), kind=kOutput, calls=%fused_computation.49 | convolution fusion | flops 1086316544 | bytes 19496960 | tf_op jit(solution)/shard_map/tkgd,skd->tkgs/dot_general | solution.py:9
  125.7 7.6 %fusion.24 = (f32[128,4,16]{0,2,1:T(8,128)S(1)}, f32[4,512,128,16]{2,1,3,0:T(8,128)}) fusion(pred[128,512]{0,1:T(8,128)(4,1)S(1)} %get-tuple-element.34, bf16[128,4,16,128]{3,2,1,0:T(8,128)(2,1)S(1)} %bitcast.322, bf16[5120,4,128]{2,0,1:T(8,128)(2,1)S(1)} %bitcast.332), kind=kOutput, calls=%fused_computation.48 | convolution fusion | flops 1086316544 | bytes 19496960 | tf_op jit(solution)/shard_map/tkgd,skd->tkgs/dot_general | solution.py:9
  133.3 7.5 %fusion.23 = (f32[128,4,16]{0,2,1:T(8,128)S(1)}, f32[4,512,128,16]{2,1,3,0:T(8,128)}) fusion(pred[128,512]{0,1:T(8,128)(4,1)S(1)} %get-tuple-element.33, bf16[128,4,16,128]{3,2,1,0:T(8,128)(2,1)S(1)} %bitcast.323, bf16[5120,4,128]{2,0,1:T(8,128)(2,1)S(1)} %bitcast.332), kind=kOutput, calls=%fused_computation.47 | convolution fusion | flops 1086316544 | bytes 19496960 | tf_op jit(solution)/shard_map/tkgd,skd->tkgs/dot_general | solution.py:9
  140.7 7.4 %fusion.22 = (f32[128,4,16]{0,2,1:T(8,128)S(1)}, f32[4,512,128,16]{2,1,3,0:T(8,128)}) fusion(pred[128,512]{0,1:T(8,128)(4,1)S(1)} %get-tuple-element.32, bf16[128,4,16,128]{3,2,1,0:T(8,128)(2,1)S(1)} %bitcast.324, bf16[5120,4,128]{2,0,1:T(8,128)(2,1)S(1)} %bitcast.332), kind=kOutput, calls=%fused_computation.46 | convolution fusion | flops 1086316544 | bytes 19496960 | tf_op jit(solution)/shard_map/tkgd,skd->tkgs/dot_general | solution.py:9
  148.1 7.6 %fusion.21 = (f32[128,4,16]{0,2,1:T(8,128)S(1)}, f32[4,512,128,16]{2,1,3,0:T(8,128)}) fusion(pred[128,512]{0,1:T(8,128)(4,1)S(1)} %get-tuple-element.31, bf16[128,4,16,128]{3,2,1,0:T(8,128)(2,1)S(1)} %bitcast.325, bf16[5120,4,128]{2,0,1:T(8,128)(2,1)S(1)} %bitcast.332), kind=kOutput, calls=%fused_computation.45 | convolution fusion | flops 1086316544 | bytes 19496960 | tf_op jit(solution)/shard_map/tkgd,skd->tkgs/dot_general | solution.py:9
  155.7 7.5 %fusion.20 = (f32[128,4,16]{0,2,1:T(8,128)S(1)}, f32[4,512,128,16]{2,1,3,0:T(8,128)}) fusion(pred[128,512]{0,1:T(8,128)(4,1)S(1)} %get-tuple-element.30, bf16[128,4,16,128]{3,2,1,0:T(8,128)(2,1)S(1)} %bitcast.316, bf16[5120,4,128]{2,0,1:T(8,128)(2,1)S(1)} %bitcast.332), kind=kOutput, calls=%fused_computation.44 | convolution fusion | flops 1086316544 | bytes 19496960 | tf_op jit(solution)/shard_map/tkgd,skd->tkgs/dot_general | solution.py:9
  163.3 7.5 %fusion.28 = (f32[128,4,16]{0,2,1:T(8,128)S(1)}, f32[4,512,128,16]{2,1,3,0:T(8,128)}) fusion(pred[128,512]{0,1:T(8,128)(4,1)S(1)} %copy-done.3, bf16[128,4,16,128]{3,2,1,0:T(8,128)(2,1)S(1)} %bitcast.318, bf16[5120,4,128]{2,0,1:T(8,128)(2,1)S(1)} %bitcast.332), kind=kOutput, calls=%fused_computation.52 | convolution fusion | flops 1086316544 | bytes 19496960 | tf_op jit(solution)/shard_map/tkgd,skd->tkgs/dot_general | solution.py:9
  170.8 7.5 %fusion.27 = (f32[128,4,16]{0,2,1:T(8,128)S(1)}, f32[4,512,128,16]{2,1,3,0:T(8,128)}) fusion(pred[128,512]{0,1:T(8,128)(4,1)S(1)} %copy-done.4, bf16[128,4,16,128]{3,2,1,0:T(8,128)(2,1)S(1)} %bitcast.319, bf16[5120,4,128]{2,0,1:T(8,128)(2,1)S(1)} %bitcast.332), kind=kOutput, calls=%fused_computation.51 | convolution fusion | flops 1086316544 | bytes 19496960 | tf_op jit(solution)/shard_map/tkgd,skd->tkgs/dot_general | solution.py:9
  178.3 7.6 %fusion.26 = (f32[128,4,16]{0,2,1:T(8,128)S(1)}, f32[4,512,128,16]{2,1,3,0:T(8,128)}) fusion(pred[128,512]{0,1:T(8,128)(4,1)S(1)} %copy-done.5, bf16[128,4,16,128]{3,2,1,0:T(8,128)(2,1)S(1)} %bitcast.320, bf16[5120,4,128]{2,0,1:T(8,128)(2,1)S(1)} %bitcast.332), kind=kOutput, calls=%fused_computation.50 | convolution fusion | flops 1086316544 | bytes 19496960 | tf_op jit(solution)/shard_map/tkgd,skd->tkgs/dot_general | solution.py:9
  185.9 7.7 %fusion.29 = (f32[128,4,16]{0,2,1:T(8,128)S(1)}, f32[4,512,128,16]{2,1,3,0:T(8,128)}) fusion(pred[128,512]{0,1:T(8,128)(4,1)S(1)} %copy-done.2, bf16[128,4,16,128]{3,2,1,0:T(8,128)(2,1)S(1)} %bitcast.317, bf16[5120,4,128]{2,0,1:T(8,128)(2,1)S(1)} %bitcast.332), kind=kOutput, calls=%fused_computation.53 | convolution fusion | flops 1086316544 | bytes 19496960 | tf_op jit(solution)/shard_map/tkgd,skd->tkgs/dot_general | solution.py:9
  193.6 9.4 %fusion = f32[128,4,16]{0,2,1:T(8,128)S(1)} fusion(f32[4,512,128,16]{2,1,3,0:T(8,128)} %get-tuple-element.59, f32[128,4,16]{0,2,1:T(8,128)S(1)} %get-tuple-element.27, pred[128,512]{0,1:T(8,128)(4,1)S(1)} %get-tuple-element.30), kind=kLoop, calls=%fused_computation.24 | loop fusion | flops 16769024 | bytes 16908288 | tf_op jit(solution)/shard_map/reduce_sum | solution.py:15
  203.0 9.4 %fusion.10 = f32[128,4,16]{0,2,1:T(8,128)S(1)} fusion(f32[4,512,128,16]{2,1,3,0:T(8,128)} %get-tuple-element.49, f32[128,4,16]{0,2,1:T(8,128)S(1)} %get-tuple-element.19, pred[128,512]{0,1:T(8,128)(4,1)S(1)} %get-tuple-element.35), kind=kLoop, calls=%fused_computation.34 | loop fusion | flops 16769024 | bytes 16908288 | tf_op jit(solution)/shard_map/reduce_sum | solution.py:15
  212.3 9.4 %fusion.2 = f32[128,4,16]{0,2,1:T(8,128)S(1)} fusion(f32[4,512,128,16]{2,1,3,0:T(8,128)} %get-tuple-element.57, f32[128,4,16]{0,2,1:T(8,128)S(1)} %get-tuple-element.23, pred[128,512]{0,1:T(8,128)(4,1)S(1)} %get-tuple-element.31), kind=kLoop, calls=%fused_computation.26 | loop fusion | flops 16769024 | bytes 16908288 | tf_op jit(solution)/shard_map/reduce_sum | solution.py:15
  221.7 9.8 %fusion.4 = f32[128,4,16]{0,2,1:T(8,128)S(1)} fusion(f32[4,512,128,16]{2,1,3,0:T(8,128)} %get-tuple-element.55, f32[128,4,16]{0,2,1:T(8,128)S(1)} %get-tuple-element.22, pred[128,512]{0,1:T(8,128)(4,1)S(1)} %get-tuple-element.32), kind=kLoop, calls=%fused_computation.28 | loop fusion | flops 16769024 | bytes 16908288 | tf_op jit(solution)/shard_map/reduce_sum | solution.py:15
  231.4 9.4 %fusion.6 = f32[128,4,16]{0,2,1:T(8,128)S(1)} fusion(f32[4,512,128,16]{2,1,3,0:T(8,128)} %get-tuple-element.53, f32[128,4,16]{0,2,1:T(8,128)S(1)} %get-tuple-element.21, pred[128,512]{0,1:T(8,128)(4,1)S(1)} %get-tuple-element.33), kind=kLoop, calls=%fused_computation.30 | loop fusion | flops 16769024 | bytes 16908288 | tf_op jit(solution)/shard_map/reduce_sum | solution.py:15
  240.8 9.4 %fusion.8 = f32[128,4,16]{0,2,1:T(8,128)S(1)} fusion(f32[4,512,128,16]{2,1,3,0:T(8,128)} %get-tuple-element.51, f32[128,4,16]{0,2,1:T(8,128)S(1)} %get-tuple-element.20, pred[128,512]{0,1:T(8,128)(4,1)S(1)} %get-tuple-element.34), kind=kLoop, calls=%fused_computation.32 | loop fusion | flops 16769024 | bytes 16908288 | tf_op jit(solution)/shard_map/reduce_sum | solution.py:15
  250.1 9.5 %fusion.12 = f32[128,4,16]{0,2,1:T(8,128)S(1)} fusion(f32[4,512,128,16]{2,1,3,0:T(8,128)} %get-tuple-element.47, f32[128,4,16]{0,2,1:T(8,128)S(1)} %get-tuple-element.18, pred[128,512]{0,1:T(8,128)(4,1)S(1)} %copy-done.5), kind=kLoop, calls=%fused_computation.36 | loop fusion | flops 16769024 | bytes 16908288 | tf_op jit(solution)/shard_map/reduce_sum | solution.py:15
  259.7 9.4 %fusion.14 = f32[128,4,16]{0,2,1:T(8,128)S(1)} fusion(f32[4,512,128,16]{2,1,3,0:T(8,128)} %get-tuple-element.45, f32[128,4,16]{0,2,1:T(8,128)S(1)} %get-tuple-element.17, pred[128,512]{0,1:T(8,128)(4,1)S(1)} %copy-done.4), kind=kLoop, calls=%fused_computation.38 | loop fusion | flops 16769024 | bytes 16908288 | tf_op jit(solution)/shard_map/reduce_sum | solution.py:15
  269.0 9.4 %fusion.16 = f32[128,4,16]{0,2,1:T(8,128)S(1)} fusion(f32[4,512,128,16]{2,1,3,0:T(8,128)} %get-tuple-element.43, f32[128,4,16]{0,2,1:T(8,128)S(1)} %get-tuple-element.16, pred[128,512]{0,1:T(8,128)(4,1)S(1)} %copy-done.3), kind=kLoop, calls=%fused_computation.40 | loop fusion | flops 16769024 | bytes 16908288 | tf_op jit(solution)/shard_map/reduce_sum | solution.py:15
  278.4 9.8 %fusion.18 = f32[128,4,16]{0,2,1:T(8,128)S(1)} fusion(f32[4,512,128,16]{2,1,3,0:T(8,128)} %get-tuple-element.41, f32[128,4,16]{0,2,1:T(8,128)S(1)} %get-tuple-element.15, pred[128,512]{0,1:T(8,128)(4,1)S(1)} %copy-done.2), kind=kLoop, calls=%fused_computation.42 | loop fusion | flops 16769024 | bytes 16908288 | tf_op jit(solution)/shard_map/reduce_sum | solution.py:15
  288.2 0.1 multiply_add_fusion
  288.3 11.9 %fusion.44 = f32[4,128,128,16]{2,1,3,0:T(8,128)} fusion(f32[4,512,128,16]{2,1,3,0:T(8,128)} %get-tuple-element.55, f32[128,4,16]{0,2,1:T(8,128)S(1)} %get-tuple-element.22, pred[128,512]{0,1:T(8,128)(4,1)S(1)} %get-tuple-element.32, bf16[5120,4,128]{0,2,1:T(8,128)(2,1)} %all-gather.5.cloned.1.call-done), kind=kOutput, calls=%fused_computation.61 | convolution fusion | flops 1090519040 | bytes 21594112 | tf_op jit(solution)/shard_map/tkgs,skd->tkgd/dot_general | solution.py:16
  300.2 11.5 %fusion.46 = f32[4,128,128,16]{2,1,3,0:T(8,128)} fusion(f32[4,512,128,16]{2,1,3,0:T(8,128)} %get-tuple-element.57, f32[128,4,16]{0,2,1:T(8,128)S(1)} %get-tuple-element.23, pred[128,512]{0,1:T(8,128)(4,1)S(1)} %get-tuple-element.31, bf16[5120,4,128]{0,2,1:T(8,128)(2,1)S(1)} %copy-done.6), kind=kOutput, calls=%fused_computation.62 | convolution fusion | flops 1090519040 | bytes 21594112 | tf_op jit(solution)/shard_map/tkgs,skd->tkgd/dot_general | solution.py:16
  311.7 11.9 %fusion.42 = f32[4,128,128,16]{2,1,3,0:T(8,128)} fusion(f32[4,512,128,16]{2,1,3,0:T(8,128)} %get-tuple-element.53, f32[128,4,16]{0,2,1:T(8,128)S(1)} %get-tuple-element.21, pred[128,512]{0,1:T(8,128)(4,1)S(1)} %get-tuple-element.33, bf16[5120,4,128]{0,2,1:T(8,128)(2,1)S(1)} %copy-done.6), kind=kOutput, calls=%fused_computation.60 | convolution fusion | flops 1090519040 | bytes 21594112 | tf_op jit(solution)/shard_map/tkgs,skd->tkgd/dot_general | solution.py:16
  323.6 11.7 %fusion.40 = f32[4,128,128,16]{2,1,3,0:T(8,128)} fusion(f32[4,512,128,16]{2,1,3,0:T(8,128)} %get-tuple-element.51, f32[128,4,16]{0,2,1:T(8,128)S(1)} %get-tuple-element.20, pred[128,512]{0,1:T(8,128)(4,1)S(1)} %get-tuple-element.34, bf16[5120,4,128]{0,2,1:T(8,128)(2,1)S(1)} %copy-done.6), kind=kOutput, calls=%fused_computation.59 | convolution fusion | flops 1090519040 | bytes 21594112 | tf_op jit(solution)/shard_map/tkgs,skd->tkgd/dot_general | solution.py:16
  335.4 5.4 %fusion.38 = f32[4,128,128,16]{2,1,3,0:T(8,128)} fusion(f32[4,512,128,16]{2,1,3,0:T(8,128)S(1)} %bitcast.329, f32[128,4,16]{0,2,1:T(8,128)S(1)} %get-tuple-element.19, pred[128,512]{0,1:T(8,128)(4,1)S(1)} %get-tuple-element.35, bf16[5120,4,128]{0,2,1:T(8,128)(2,1)S(1)} %copy-done.6), kind=kOutput, calls=%fused_computation.58 | convolution fusion | flops 1090519040 | bytes 21594112 | tf_op jit(solution)/shard_map/tkgs,skd->tkgd/dot_general | solution.py:16
  340.8 11.5 %fusion.36 = f32[4,128,128,16]{2,1,3,0:T(8,128)} fusion(f32[4,512,128,16]{2,1,3,0:T(8,128)} %get-tuple-element.47, f32[128,4,16]{0,2,1:T(8,128)S(1)} %get-tuple-element.18, pred[128,512]{0,1:T(8,128)(4,1)S(1)} %copy-done.5, bf16[5120,4,128]{0,2,1:T(8,128)(2,1)S(1)} %copy-done.6), kind=kOutput, calls=%fused_computation.57 | convolution fusion | flops 1090519040 | bytes 21594112 | tf_op jit(solution)/shard_map/tkgs,skd->tkgd/dot_general | solution.py:16
  352.3 11.6 %fusion.34 = f32[4,128,128,16]{2,1,3,0:T(8,128)} fusion(f32[4,512,128,16]{2,1,3,0:T(8,128)} %get-tuple-element.45, f32[128,4,16]{0,2,1:T(8,128)S(1)} %get-tuple-element.17, pred[128,512]{0,1:T(8,128)(4,1)S(1)} %copy-done.4, bf16[5120,4,128]{0,2,1:T(8,128)(2,1)S(1)} %copy-done.6), kind=kOutput, calls=%fused_computation.56 | convolution fusion | flops 1090519040 | bytes 21594112 | tf_op jit(solution)/shard_map/tkgs,skd->tkgd/dot_general | solution.py:16
  363.9 11.7 %fusion.32 = f32[4,128,128,16]{2,1,3,0:T(8,128)} fusion(f32[4,512,128,16]{2,1,3,0:T(8,128)} %get-tuple-element.43, f32[128,4,16]{0,2,1:T(8,128)S(1)} %get-tuple-element.16, pred[128,512]{0,1:T(8,128)(4,1)S(1)} %copy-done.3, bf16[5120,4,128]{0,2,1:T(8,128)(2,1)S(1)} %copy-done.6), kind=kOutput, calls=%fused_computation.55 | convolution fusion | flops 1090519040 | bytes 21594112 | tf_op jit(solution)/shard_map/tkgs,skd->tkgd/dot_general | solution.py:16
  375.6 12.1 %fusion.30 = f32[4,128,128,16]{2,1,3,0:T(8,128)} fusion(f32[4,512,128,16]{2,1,3,0:T(8,128)} %get-tuple-element.41, f32[128,4,16]{0,2,1:T(8,128)S(1)} %get-tuple-element.15, pred[128,512]{0,1:T(8,128)(4,1)S(1)} %copy-done.2, bf16[5120,4,128]{0,2,1:T(8,128)(2,1)} %all-gather.5.cloned.1.call-done), kind=kOutput, calls=%fused_computation.54 | convolution fusion | flops 1090519040 | bytes 21594112 | tf_op jit(solution)/shard_map/tkgs,skd->tkgd/dot_general | solution.py:16
  387.7 15.7 %fusion.61 = bf16[128,4,16,128]{0,3,2,1:T(8,128)(2,1)} fusion(f32[4,128,128,16]{2,1,3,0:T(8,128)} %fusion.30, f32[4,128,128,16]{2,1,3,0:T(8,128)} %fusion.32, f32[4,128,128,16]{2,1,3,0:T(8,128)} %fusion.34, f32[4,128,128,16]{2,1,3,0:T(8,128)} %fusion.36, f32[4,128,128,16]{2,1,3,0:T(8,128)} %fusion.38, f32[4,128,128,16]{2,1,3,0:T(8,128)} %fusion.40, ...), kind=kOutput, calls=%fused_computation.76 | convolution fusion | flops 1112539136 | bytes 57606144 | tf_op jit(solution)/shard_map/tkgs,skd->tkgd/dot_general | solution.py:16
  403.5 4.1 copy.182
  (63 shorter events, 0.4 us)
Async XLA Ops:
  6.5 108.9 %copy-start = (bf16[1,128,64,128]{3,2,1,0:T(8,128)(2,1)S(1)}, bf16[1,128,64,128]{3,2,1,0:T(8,128)(2,1)}, u32[]{:S(2)}) copy-start(bf16[1,128,64,128]{3,2,1,0:T(8,128)(2,1)} %param.8) | copy-start | bytes 6291460
  20.4 16.5 %all-to-all-start = ((bf16[16,1,32,4,128]{4,2,3,1,0:T(8,128)(2,1)}), bf16[16,1,32,4,128]{4,2,3,1,0:T(8,128)(2,1)S(1)}, u32[]{:S(2)}, u32[]{:S(2)}) async-start(bf16[16,1,32,4,128]{4,2,3,1,0:T(8,128)(2,1)} %get-tuple-element.29), calls=%async_computation | async-start | bytes 1048576 | tf_op jit(solution)/shard_map/all_to_all | solution.py:65
  26.0 89.4 %all-gather.3.cloned.1.call-start = ((), (), s32[]{:S(2)}) async-start(), calls=%async_computation.2 | async-start | bytes 5898240 | tf_op jit(solution)/shard_map/all_gather | solution.py:81
  38.5 14.6 %all-to-all-start.1 = ((bf16[16,1,32,4,128]{4,2,3,1,0:T(8,128)(2,1)}), bf16[16,1,32,4,128]{4,2,3,1,0:T(8,128)(2,1)S(1)}, u32[]{:S(2)}, u32[]{:S(2)}) async-start(bf16[16,1,32,4,128]{4,2,3,1,0:T(8,128)(2,1)} %get-tuple-element.28), calls=%async_computation.1 | async-start | bytes 1048576 | tf_op jit(solution)/shard_map/all_to_all | solution.py:66
  42.1 246.2 %all-gather.5.cloned.1.call-start = ((), (), s32[]{:S(2)}) async-start(), calls=%async_computation.3 | async-start | bytes 5898240 | tf_op jit(solution)/shard_map/all_gather | solution.py:82
  115.4 10.3 %slice-start.8 = ((s8[5242880]{0:T(1024)(128)(4,1)}), s8[4194304]{0:T(1024)(128)(4,1)S(1)}, s32[]{:S(2)}) async-start(s8[5242880]{0:T(1024)(128)(4,1)} %bitcast.331), calls=%async_computation.12 | async-start | bytes 8388608
  115.4 10.3 %slice-start.9 = ((s8[5242880]{0:T(1024)(128)(4,1)}), s8[1048576]{0:T(1024)(128)(4,1)S(1)}, s32[]{:S(2)}) async-start(s8[5242880]{0:T(1024)(128)(4,1)} %bitcast.331), calls=%async_computation.13 | async-start | bytes 2097152
  148.1 15.2 %copy-start.3 = (pred[128,512]{0,1:T(8,128)(4,1)S(1)}, pred[128,512]{0,1:T(8,128)(4,1)}, u32[]{:S(2)}) copy-start(pred[128,512]{0,1:T(8,128)(4,1)} %get-tuple-element.38) | copy-start | bytes 196612
  155.7 15.0 %copy-start.4 = (pred[128,512]{0,1:T(8,128)(4,1)S(1)}, pred[128,512]{0,1:T(8,128)(4,1)}, u32[]{:S(2)}) copy-start(pred[128,512]{0,1:T(8,128)(4,1)} %get-tuple-element.37) | copy-start | bytes 196612
  163.3 15.0 %copy-start.5 = (pred[128,512]{0,1:T(8,128)(4,1)S(1)}, pred[128,512]{0,1:T(8,128)(4,1)}, u32[]{:S(2)}) copy-start(pred[128,512]{0,1:T(8,128)(4,1)} %get-tuple-element.36) | copy-start | bytes 196612
  170.8 15.1 %copy-start.2 = (pred[128,512]{0,1:T(8,128)(4,1)S(1)}, pred[128,512]{0,1:T(8,128)(4,1)}, u32[]{:S(2)}) copy-start(pred[128,512]{0,1:T(8,128)(4,1)} %get-tuple-element.39) | copy-start | bytes 196612
  288.3 11.9 %copy-start.6 = (bf16[5120,4,128]{0,2,1:T(8,128)(2,1)S(1)}, bf16[5120,4,128]{0,2,1:T(8,128)(2,1)}, u32[]{:S(2)}) copy-start(bf16[5120,4,128]{0,2,1:T(8,128)(2,1)} %all-gather.5.cloned.1.call-done) | copy-start | bytes 15728644
  311.7 23.6 %slice-start.4 = ((s8[16777216]{0:T(1024)(128)(4,1)}), s8[4194304]{0:T(1024)(128)(4,1)S(1)}, s32[]{:S(2)}) async-start(s8[16777216]{0:T(1024)(128)(4,1)} %bitcast.328), calls=%async_computation.8 | async-start | bytes 8388608
  311.7 23.6 %slice-start.5 = ((s8[16777216]{0:T(1024)(128)(4,1)}), s8[4194304]{0:T(1024)(128)(4,1)S(1)}, s32[]{:S(2)}) async-start(s8[16777216]{0:T(1024)(128)(4,1)} %bitcast.328), calls=%async_computation.9 | async-start | bytes 8388608
  323.6 11.7 %slice-start.6 = ((s8[16777216]{0:T(1024)(128)(4,1)}), s8[4194304]{0:T(1024)(128)(4,1)S(1)}, s32[]{:S(2)}) async-start(s8[16777216]{0:T(1024)(128)(4,1)} %bitcast.328), calls=%async_computation.10 | async-start | bytes 8388608
  323.6 11.7 %slice-start.7 = ((s8[16777216]{0:T(1024)(128)(4,1)}), s8[4194304]{0:T(1024)(128)(4,1)S(1)}, s32[]{:S(2)}) async-start(s8[16777216]{0:T(1024)(128)(4,1)} %bitcast.328), calls=%async_computation.11 | async-start | bytes 8388608
  363.9 23.8 %slice-start = ((s8[16777216]{0:T(1024)(128)(4,1)}), s8[4194304]{0:T(1024)(128)(4,1)S(1)}, s32[]{:S(2)}) async-start(s8[16777216]{0:T(1024)(128)(4,1)} %bitcast.326), calls=%async_computation.4 | async-start | bytes 8388608
  363.9 23.8 %slice-start.1 = ((s8[16777216]{0:T(1024)(128)(4,1)}), s8[4194304]{0:T(1024)(128)(4,1)S(1)}, s32[]{:S(2)}) async-start(s8[16777216]{0:T(1024)(128)(4,1)} %bitcast.326), calls=%async_computation.5 | async-start | bytes 8388608
  375.6 12.1 %slice-start.2 = ((s8[16777216]{0:T(1024)(128)(4,1)}), s8[4194304]{0:T(1024)(128)(4,1)S(1)}, s32[]{:S(2)}) async-start(s8[16777216]{0:T(1024)(128)(4,1)} %bitcast.326), calls=%async_computation.6 | async-start | bytes 8388608
  375.6 12.1 %slice-start.3 = ((s8[16777216]{0:T(1024)(128)(4,1)}), s8[4194304]{0:T(1024)(128)(4,1)S(1)}, s32[]{:S(2)}) async-start(s8[16777216]{0:T(1024)(128)(4,1)} %bitcast.326), calls=%async_computation.7 | async-start | bytes 8388608
  387.7 19.9 %copy-start.1 = (bf16[1,128,64,128]{3,2,1,0:T(8,128)(2,1)S(1)}, bf16[1,128,64,128]{3,2,1,0:T(8,128)(2,1)}, u32[]{:S(2)}) copy-start(bf16[1,128,64,128]{3,2,1,0:T(8,128)(2,1)} %param.8) | copy-start | bytes 6291460
Sparse Core Ops, SparseCore 0:
  38.6 76.7 all-gather.2
  117.7 77.7 all-gather.4
where the time goes:
time: 422 us; the launch traced here: 415 us
  matrix products  193 us (46%)
  other arithmetic  110 us (26%)
  waiting for transfers between devices  67.6 us (16%)
  local copies, waits for them, and re-layouts  20.5 us (5%)
  between operations  14 us (3%)
  starting transfers between devices  9.82 us (2%)
    dot_general x10, matrix products, attend(): jnp.einsum('tkgs,skd->tkgd', weights.astype(jnp.bfloat16), values, prefer...  115 us
    reduce_sum x10, other arithmetic, attend(): total = total * factor + jnp.sum(weights, axis=-1)  94.5 us
    dot_general x10, matrix products, attend(): jnp.einsum('tkgd,skd->tkgs', query_groups, keys, preferred_element_type=j...  78.1 us
    all_gather x1, waiting for transfers between devices, per_device(): lax.all_gather(block_keys, 'ctx', axis=0, tiled=True)  57.7 us
    all_to_all x1, waiting for transfers between devices, per_device(): lax.all_to_all(send_keys, 'req', split_axis=0, concat_axis=0, tiled=True)  9.85 us
  transfers between devices with their start and end apart: 4, of which 2 were waited for; matrix products, arithmetic and copies ran while one was open for 45% of the time, Pallas kernels for 0%

commit v1 on v0

v1 whole, which is shorter than its diff:
```python
import functools

import jax
import jax.numpy as jnp
from jax import lax
from jax.experimental import pallas as pl
from jax.experimental.pallas import tpu as pltpu
from jax.sharding import PartitionSpec as P

MESH = pl.DeviceIdType.MESH
F32 = jnp.float32
BF16 = jnp.bfloat16
NT = (((1,), (1,)), ((), ()))
NN = (((1,), (0,)), ((), ()))
DEAD = 448.0
LOG2E = 1.4426950408889634
ROWS = 256
CHUNK = 1024


def pack_kernel(
    dims, hits, counts, home, sk_hbm, sv_hbm, stk_hbm, stv_hbm, send, span_send,
    slots, lives, store, span_in, local_sem,
):
    n_req, n_ctx, heads, store_dev, page_len, tokens, group, hd = dims
    piece = page_len * heads
    me_req = lax.axis_index("req")
    me_ctx = lax.axis_index("ctx")

    load_k = pltpu.make_async_copy(stk_hbm, store.at[0], local_sem.at[0])
    load_v = pltpu.make_async_copy(stv_hbm, store.at[1], local_sem.at[1])
    load_sk = pltpu.make_async_copy(sk_hbm, span_in.at[0], local_sem.at[2])
    load_sv = pltpu.make_async_copy(sv_hbm, span_in.at[1], local_sem.at[3])
    load_sk.start()
    load_sv.start()
    load_k.start()
    load_v.start()

    def find(r, _):
        slot = jnp.int32(0)
        live = jnp.int32(0)
        for i in range(n_req):
            j = i * n_ctx + me_ctx
            row = home[0, hits[r, j]]
            mine = lax.div(row, store_dev) == me_req
            slot = jnp.where(mine, lax.rem(row, store_dev), slot)
            live = jnp.where(mine, (j < counts[r]).astype(jnp.int32), live)
        slots[r] = slot
        lives[r] = live
        return 0

    lax.fori_loop(0, n_req, find, 0)

    to = lax.broadcasted_iota(jnp.int32, (piece, piece), 0)
    frm = lax.broadcasted_iota(jnp.int32, (piece, piece), 1)
    swap = (lax.rem(to, page_len) * heads + lax.div(to, page_len) == frm).astype(F32).astype(BF16)

    load_sk.wait()
    load_sv.wait()
    for g in range(tokens // page_len):
        pair = jnp.concatenate(
            [span_in[0, g * piece : (g + 1) * piece, :], span_in[1, g * piece : (g + 1) * piece, :]], axis=1
        )
        moved = lax.dot_general(swap, pair, NN, preferred_element_type=F32).astype(BF16)
        for h in range(heads):
            span_send[h, g * page_len : (g + 1) * page_len, :] = moved[h * page_len : (h + 1) * page_len, :]
    load_k.wait()
    load_v.wait()

    def pack(r, _):
        at = pl.ds(pl.multiple_of(slots[r] * piece, piece), piece)
        live = lives[r] > 0
        pair = jnp.concatenate([store[0, at, :], store[1, at, :]], axis=1)
        moved = lax.dot_general(swap, pair, NN, preferred_element_type=F32)
        lane = lax.broadcasted_iota(jnp.int32, (1, 2 * hd), 1)
        filler = jnp.where(lane < hd, DEAD, 0.0)
        moved = jnp.where(live, moved, jnp.broadcast_to(filler, moved.shape)).astype(BF16)
        for h in range(heads):
            send[r, h] = moved[h * page_len : (h + 1) * page_len, :]
        return 0

    lax.fori_loop(0, n_req, pack, 0)


def kernel(
    dims, q_hbm, send, span_send, out_hbm, qbuf, kv, acc, peak, ostage,
    own_sem, page_send, page_recv, span_sent, span_recv, q_sent, q_recv, o_sent, o_recv,
):
    n_req, n_ctx, heads, store_dev, page_len, tokens, group, hd = dims
    rows = tokens * group
    prefix = n_req * n_ctx * page_len
    me_req = lax.axis_index("req")
    me_ctx = lax.axis_index("ctx")
    col = lax.rem(me_ctx, heads)
    half = lax.div(me_ctx, heads)
    scale = hd ** -0.5 * LOG2E

    barrier = pltpu.get_barrier_semaphore()
    n_dev = n_req * n_ctx

    def greet(o, _):
        req = lax.rem(me_req + lax.div(o, n_ctx), n_req)
        ctx = lax.rem(me_ctx + lax.rem(o, n_ctx), n_ctx)
        pl.semaphore_signal(barrier, inc=1, device_id=(req, ctx), device_id_type=MESH)
        return 0

    lax.fori_loop(1, n_dev, greet, 0)
    pl.semaphore_wait(barrier, n_dev - 1)

    span_at = pl.ds(pl.multiple_of(prefix + me_ctx * tokens, tokens), tokens)
    span_dst = kv.at[span_at, pl.ds(0, 2 * hd)]
    pltpu.make_async_copy(span_send.at[col], span_dst, span_recv).start()

    def send_span(o, _):
        ctx = lax.rem(me_ctx + o, n_ctx)
        pltpu.make_async_remote_copy(
            span_send.at[lax.rem(ctx, heads)], span_dst, span_sent, span_recv,
            device_id=(me_req, ctx), device_id_type=MESH,
        ).start()
        return 0

    lax.fori_loop(1, n_ctx, send_span, 0)
    page_at = pl.ds(pl.multiple_of((me_ctx * n_req + me_req) * page_len, page_len), page_len)
    page_dst = kv.at[page_at, pl.ds(0, 2 * hd)]
    pltpu.make_async_copy(send.at[me_req, col], page_dst, page_recv.at[me_ctx]).start()

    def send_page(o, _):
        dc = lax.div(o, n_req)
        req = lax.rem(me_req + lax.rem(o, n_req), n_req)
        ctx = lax.rem(me_ctx + dc, n_ctx)
        pltpu.make_async_remote_copy(
            send.at[req, lax.rem(ctx, heads)], page_dst, page_send, page_recv.at[me_ctx],
            device_id=(req, ctx), device_id_type=MESH,
        ).start()
        return 0

    def q_src(c):
        return q_hbm.at[:, pl.ds(pl.multiple_of(c * group, group), group), :]

    pltpu.make_async_copy(q_src(col), qbuf.at[0], q_recv.at[0]).start()
    lax.fori_loop(1, n_dev, send_page, 0)

    def send_q(o, _):
        to_col = lax.rem(col + o, heads)
        pltpu.make_async_remote_copy(
            q_src(to_col), qbuf.at[o], q_sent, q_recv.at[o],
            device_id=(me_req, half * heads + to_col), device_id_type=MESH,
        ).start()
        return 0

    lax.fori_loop(1, heads, send_q, 0)

    def whole(ref, sem):
        return pltpu.make_async_copy(ref, ref, sem)

    whole(kv.at[pl.ds(prefix, n_ctx * tokens), pl.ds(0, 2 * hd)], span_recv).wait()
    kv[prefix : prefix + n_ctx * tokens, 2 * hd :] = jnp.ones((n_ctx * tokens, hd), BF16)
    per_slot = n_req * page_len

    def settle(c):
        at = pl.ds(pl.multiple_of(c * per_slot, per_slot), per_slot)
        whole(kv.at[at, pl.ds(0, 2 * hd)], page_recv.at[c]).wait()
        key0 = kv[prefix : prefix + 16, 0:hd].astype(F32)[0:1, :]
        raw = kv[at, 0:hd].astype(F32)
        dead = raw > 100.0
        kv[at, 0:hd] = jnp.where(dead, key0, raw).astype(BF16)
        kv[at, 2 * hd :] = jnp.where(dead, 0.0, 1.0).astype(BF16)

    def attend(dx, start, size, first_token):
        at = pl.ds(start, size)
        tiles = rows // ROWS
        toks = ROWS // group

        def score(t):
            q = qbuf[dx, t * toks : (t + 1) * toks].reshape(ROWS, hd)
            return lax.dot_general(q, kv[at, 0:hd], NT, preferred_element_type=F32)

        following = score(0)
        for t in range(tiles):
            s = following * scale
            if t + 1 < tiles:
                following = score(t + 1)
            if first_token is not None:
                token = lax.broadcasted_iota(jnp.int32, (ROWS, size), 0) // group + (first_token + t * toks)
                key = lax.broadcasted_iota(jnp.int32, (ROWS, size), 1)
                s = jnp.where(key <= token, s, -1e30)
            r = slice(t * ROWS, (t + 1) * ROWS)
            before = peak[r, :]
            now = jnp.maximum(before, jnp.max(s, axis=1, keepdims=True))
            peak[r, :] = now
            factor = jnp.exp2(before - now)
            w = jnp.exp2(s - jnp.concatenate([now] * (size // hd), axis=1)).astype(BF16)
            wv = lax.dot_general(w, kv[at, hd:], NN, preferred_element_type=F32)
            acc[r, :] = acc[r, :] * jnp.concatenate([factor, factor], axis=1) + wv

    def block(dx, _):
        whole(qbuf.at[dx], q_recv.at[dx]).wait()
        acc[...] = jnp.zeros_like(acc)
        peak[...] = jnp.full(peak.shape, -1e30, F32)
        from_col = lax.rem(col - dx + heads, heads)
        first = (half * heads + from_col) * tokens

        slots_per = CHUNK // per_slot

        def chunk(i, _):
            c = lax.rem(lax.div(me_ctx, slots_per) + n_ctx // slots_per - i, n_ctx // slots_per)

            @pl.when(dx == 0)
            def _():
                for u in range(slots_per):
                    settle(c * slots_per + u)

            attend(dx, pl.multiple_of(c * CHUNK, CHUNK), CHUNK, None)
            return 0

        lax.fori_loop(0, prefix // CHUNK, chunk, 0)
        for z in range(n_ctx // heads):

            @pl.when(half == z)
            def _():
                attend(dx, prefix, (z + 1) * heads * tokens, first)

        out = acc[:, 0:hd] / acc[:, hd:]
        ostage[dx] = out.astype(BF16).reshape(tokens, group, hd)
        o_dst = out_hbm.at[:, pl.ds(pl.multiple_of(col * group, group), group), :]

        @pl.when(dx == 0)
        def _():
            pltpu.make_async_copy(ostage.at[dx], o_dst, own_sem).start()

        @pl.when(dx > 0)
        def _():
            pltpu.make_async_remote_copy(
                ostage.at[dx], o_dst, o_sent, o_recv,
                device_id=(me_req, half * heads + from_col), device_id_type=MESH,
            ).start()

        return 0

    lax.fori_loop(0, heads, block, 0)
    pltpu.make_async_copy(ostage.at[0], ostage.at[0], own_sem).wait()
    whole(kv.at[pl.ds(0, (n_ctx - 1) * tokens), pl.ds(0, 2 * hd)], span_sent).wait()
    whole(kv.at[pl.ds(0, (n_dev - 1) * page_len), pl.ds(0, 2 * hd)], page_send).wait()
    whole(qbuf.at[pl.ds(0, heads - 1)], q_sent).wait()
    whole(ostage.at[pl.ds(0, heads - 1)], o_sent).wait()
    whole(ostage.at[pl.ds(0, heads - 1)], o_recv).wait()


def per_device(queries, span_keys, span_values, store_keys, store_values, page_home, hits, counts):
    n_req = lax.axis_size("req")
    n_ctx = lax.axis_size("ctx")
    _, tokens, q_heads, hd = queries.shape
    heads = span_keys.shape[2]
    group = q_heads // heads
    _, store_dev, page_len, _, _ = store_keys.shape
    dims = (n_req, n_ctx, heads, store_dev, page_len, tokens, group, hd)
    rows = tokens * group
    keys = n_req * n_ctx * page_len + n_ctx * tokens
    smem = pl.BlockSpec(memory_space=pltpu.SMEM)
    hbm = pl.BlockSpec(memory_space=pl.ANY)
    dma = pltpu.SemaphoreType.DMA
    vmem = pl.BlockSpec(memory_space=pltpu.VMEM)
    send, span_send = pl.pallas_call(
        functools.partial(pack_kernel, dims),
        out_shape=(
            jax.ShapeDtypeStruct((n_req, heads, page_len, 2 * hd), BF16),
            jax.ShapeDtypeStruct((heads, tokens, 2 * hd), BF16),
        ),
        in_specs=[smem] * 3 + [hbm] * 4,
        out_specs=(vmem, vmem),
        scratch_shapes=[
            pltpu.SMEM((n_req,), jnp.int32),
            pltpu.SMEM((n_req,), jnp.int32),
            pltpu.VMEM((2, store_dev * page_len * heads, hd), BF16),
            pltpu.VMEM((2, tokens * heads, hd), BF16),
            dma((4,)),
        ],
        compiler_params=pltpu.CompilerParams(vmem_limit_bytes=32 * 2**20),
        name="pack_pages",
    )(
        hits, counts, page_home,
        span_keys.reshape(tokens * heads, hd),
        span_values.reshape(tokens * heads, hd),
        store_keys.reshape(store_dev * page_len * heads, hd),
        store_values.reshape(store_dev * page_len * heads, hd),
    )
    out = pl.pallas_call(
        functools.partial(kernel, dims),
        out_shape=jax.ShapeDtypeStruct((tokens, q_heads, hd), BF16),
        in_specs=[hbm] * 3,
        out_specs=hbm,
        scratch_shapes=[
            pltpu.VMEM((heads, tokens, group, hd), BF16),
            pltpu.VMEM((keys, 3 * hd), BF16),
            pltpu.VMEM((rows, 2 * hd), F32),
            pltpu.VMEM((rows, hd), F32),
            pltpu.VMEM((heads, tokens, group, hd), BF16),
            dma,
            dma,
            dma((n_ctx,)),
            dma,
            dma,
            dma,
            dma((heads,)),
            dma,
            dma,
        ],
        compiler_params=pltpu.CompilerParams(
            collective_id=0, has_side_effects=True, vmem_limit_bytes=60 * 2**20
        ),
        name="attend_pages",
    )(queries[0], send, span_send)
    return out[None]


def solution(mesh):
    placed = (
        P("req", "ctx", None, None),
        P("req", "ctx", None, None),
        P("req", "ctx", None, None),
        P("ctx", "req", None, None, None),
        P("ctx", "req", None, None, None),
        P("ctx", None),
        P(),
        P(),
    )
    return jax.shard_map(
        per_device,
        mesh=mesh,
        in_specs=placed,
        out_specs=P("req", "ctx", None, None),
        check_vma=False,
    )
```

time: 422 us -> 137 us (0.32); the launches traced: 415 us -> 136 us
  matrix products: 193 us -> 0 us
  Pallas kernels: 0 us -> 125 us
  other arithmetic: 110 us -> 0 us
  waiting for transfers between devices: 67.6 us -> 0 us
  between operations: 14 us -> 0.03 us
  starting transfers between devices: 9.82 us -> 0 us
  local copies, waits for them, and re-layouts: 20.5 us -> 11 us
    dot_general x20 -> x0, matrix products: 193 us -> none  [the longest x10 115 us: attend(): jnp.einsum('tkgs,skd->tkgd', weights.astype(jnp.bfloat16), values, prefer...]
    pallas_call x0 -> x2, Pallas kernels: none -> 125 us  [the longest x1 120 us: per_device(): pl.pallas_call(functools.partial(kernel, dims), out_shape=jax.ShapeDtypeS...]
    reduce_sum x13 -> x0, other arithmetic: 96.2 us -> none  [the longest x10 94.5 us: attend(): total = total * factor + jnp.sum(weights, axis=-1)]
    all_gather x2 -> x0, waiting for transfers between devices: 57.8 us -> none  [the longest x1 57.7 us: per_device(): lax.all_gather(block_keys, 'ctx', axis=0, tiled=True)]
    all_to_all x2 -> x0, waiting for transfers between devices: 9.85 us -> none  [the longest x1 9.85 us: per_device(): lax.all_to_all(send_keys, 'req', split_axis=0, concat_axis=0, tiled=True)]
    all_to_all x2 -> x0, starting transfers between devices: 9.22 us -> none  [the longest x1 5.63 us: per_device(): lax.all_to_all(send_keys, 'req', split_axis=0, concat_axis=0, tiled=True)]
    gather x6 -> x0, local copies, waits for them, and re-layouts: 6.24 us -> none  [the longest x1 2.65 us: per_device(): store_keys[0][local_slot]]
    select_n x6 -> x0, other arithmetic: 5.99 us -> none  [the longest x2 3.65 us: per_device(): jnp.where(is_prefix[None, :], page_live[None, :], key_pos[None, :] <= que...]
  transfers between devices with their start and end apart: 4 -> 0, of which waited for: 2 -> 0; matrix products, arithmetic and copies ran while one was open for 45% -> 0% of each run, Pallas kernels for 0% -> 0%
where the time goes in v1:
time: 137 us; the launch traced here: 136 us
  Pallas kernels  125 us (91%)
  local copies, waits for them, and re-layouts  11 us (8%)
    pallas_call x1, Pallas kernels, per_device(): pl.pallas_call(functools.partial(kernel, dims), out_shape=jax.ShapeDtypeS...  120 us
    unnamed x19, local copies, waits for them, and re-layouts  11 us
    pallas_call x1, Pallas kernels, per_device(): pl.pallas_call(functools.partial(pack_kernel, dims), out_shape=(jax.Shape...  5.53 us

profile of v1, /device:TPU:64, one launch (start us, length us, event | category | flops | bytes accessed | tf_op | source)
XLA Modules:
  0.0 136.1 jit_solution(17520950984905562417)
XLA Ops:
  0.0 0.0 copy-start
  0.0 1.2 copy-done
  1.2 0.0 copy-start.1
  1.2 1.2 copy-done.1
  2.5 0.0 copy-start.4
  2.5 0.9 copy-done.4
  3.4 0.0 copy-start.5
  3.4 0.9 copy-done.5
  4.3 0.0 copy-start.6
  4.3 0.7 copy-done.6
  5.0 0.0 copy-start.7
  5.0 0.7 copy-done.7
  5.6 0.0 copy-start.8
  5.6 0.7 copy-done.8
  6.3 5.5 %pack_pages.1 = (bf16[16,4,32,256]{3,2,1,0:T(8,128)(2,1)S(1)}, bf16[4,128,256]{2,1,0:T(8,128)(2,1)S(1)}) custom-call(s32[16,128]{1,0:T(8,128)S(1)} %copy-done.6, s32[16]{0:T(128)S(1)} %copy-done.8, s32[1,512]{1,0:T(1,128)S(1)} %copy-done.7, bf16[512,128]{1,0:T(8,128)(2,1)S(1)} %bitcast.8, bf16[512,128]{1,0:T(8,128)(2,1)S(1)} %bitcast.9, ...), custom_call_target="tpu_custom_call" | custom-call | tf_op jit(solution)/shard_map/pack_pages/pallas_call | solution.py:263
  11.8 0.0 copy-start.2
  11.8 1.0 copy-done.2
  12.8 0.0 copy-start.3
  12.8 0.7 copy-done.3
  13.5 119.5 %attend_pages.1 = bf16[128,64,128]{2,1,0:T(8,128)(2,1)} custom-call(bf16[128,64,128]{2,1,0:T(8,128)(2,1)} %bitcast.11, bf16[16,4,32,256]{3,2,1,0:T(8,128)(2,1)} %copy-done.2, bf16[4,128,256]{2,1,0:T(8,128)(2,1)} %copy-done.3), custom_call_target="tpu_custom_call" | custom-call | tf_op jit(solution)/shard_map/attend_pages/pallas_call | solution.py:287
  133.0 3.1 %copy.10 = bf16[1,128,64,128]{3,2,1,0:T(8,128)(2,1)} copy(bf16[1,128,64,128]{3,2,1,0:T(8,128)(2,1)} %bitcast.10) | data formatting | bytes 4194304
Async XLA Ops:
  0.0 1.2 copy-start
  1.2 1.2 copy-start.1
  2.5 0.9 copy-start.4
  3.4 0.9 copy-start.5
  4.3 0.7 copy-start.6
  5.0 0.7 copy-start.7
  5.6 0.7 copy-start.8
  11.8 1.0 copy-start.2
  12.8 0.7 copy-start.3

commit v2 on v0

v2 whole, which is shorter than its diff:
```python
import functools

import jax
import jax.numpy as jnp
from jax import lax
from jax.experimental import pallas as pl
from jax.experimental.pallas import tpu as pltpu
from jax.sharding import PartitionSpec as P

MESH = pl.DeviceIdType.MESH
F32 = jnp.float32
BF16 = jnp.bfloat16
NT = (((1,), (1,)), ((), ()))
NN = (((1,), (0,)), ((), ()))
DEAD = 448.0
LOG2E = 1.4426950408889634
ROWS = 256


def kernel(
    dims, hits, counts, home, q_hbm, sk_hbm, sv_hbm, stk_hbm, stv_hbm, out_hbm,
    store, span_in, send, span_send, qbuf, raw, kv, acc, peak, ostage,
    load_sem, page_sent, page_recv, span_sent, span_recv, pass_sent, pass_recv,
    span_pass_sent, span_pass_recv, q_sent, q_recv, o_sent, o_recv, own_sem,
):
    n_req, n_ctx, heads, store_dev, page_len, tokens, group, hd = dims
    halves = n_ctx // heads
    part = tokens // 2
    piece = page_len * heads
    per_slot = n_req * page_len
    near = heads * per_slot
    prefix = halves * near
    span = heads * tokens
    me_req = lax.axis_index("req")
    me_ctx = lax.axis_index("ctx")
    col = lax.rem(me_ctx, heads)
    half = lax.div(me_ctx, heads)
    partner = (me_req, (1 - half) * heads + col)
    scale = hd ** -0.5 * LOG2E
    both = pl.ds(0, 2 * hd)

    loads = [
        pltpu.make_async_copy(src, dst, load_sem.at[i])
        for i, (src, dst) in enumerate(
            [(sk_hbm, span_in.at[0]), (sv_hbm, span_in.at[1]), (stk_hbm, store.at[0]), (stv_hbm, store.at[1])]
        )
    ]
    for load in loads:
        load.start()

    def whole(ref, sem):
        return pltpu.make_async_copy(ref, ref, sem)

    def q_src(c, h):
        return q_hbm.at[pl.ds(h * part, part), pl.ds(pl.multiple_of(c * group, group), group), :]

    for h in range(2):
        pltpu.make_async_copy(q_src(col, h), qbuf.at[h], q_recv.at[h]).start()

    barrier = pltpu.get_barrier_semaphore()

    def near_device(o):
        req = lax.rem(me_req + lax.div(o, heads), n_req)
        return req, half * heads + lax.rem(col + lax.rem(o, heads), heads)

    def greet(o, _):
        pl.semaphore_signal(barrier, inc=1, device_id=near_device(o), device_id_type=MESH)
        return 0

    lax.fori_loop(1, n_req * heads, greet, 0)
    pl.semaphore_signal(barrier, inc=1, device_id=partner, device_id_type=MESH)

    to = lax.broadcasted_iota(jnp.int32, (piece, piece), 0)
    frm = lax.broadcasted_iota(jnp.int32, (piece, piece), 1)
    swap = (lax.rem(to, page_len) * heads + lax.div(to, page_len) == frm).astype(F32).astype(BF16)

    for load in loads[:2]:
        load.wait()
    for g in range(tokens // page_len):
        pair = jnp.concatenate(
            [span_in[0, g * piece : (g + 1) * piece, :], span_in[1, g * piece : (g + 1) * piece, :]], axis=1
        )
        moved = lax.dot_general(swap, pair, NN, preferred_element_type=F32).astype(BF16)
        for h in range(heads):
            span_send[h, g * page_len : (g + 1) * page_len, :] = moved[h * page_len : (h + 1) * page_len, :]
    for load in loads[2:]:
        load.wait()

    def pack(r, _):
        slot = jnp.int32(0)
        live = jnp.int32(0)
        for i in range(n_req):
            j = i * n_ctx + me_ctx
            row = home[0, hits[r, j]]
            mine = (lax.div(row, store_dev) == me_req).astype(jnp.int32)
            slot = slot + mine * lax.rem(row, store_dev)
            live = live + mine * (j < counts[r]).astype(jnp.int32)
        live = live.astype(F32)
        pair = jnp.concatenate([store[0, slot], store[1, slot]], axis=1)
        moved = lax.dot_general(swap, pair, NN, preferred_element_type=F32)
        lane = lax.broadcasted_iota(jnp.int32, moved.shape, 1)
        filler = jnp.where(lane < hd, DEAD, 0.0)
        moved = (moved * live + filler * (1.0 - live)).astype(BF16)
        for h in range(heads):
            send[r, h] = moved[h * page_len : (h + 1) * page_len, :]
        return 0

    lax.fori_loop(0, n_req, pack, 0)
    pl.semaphore_wait(barrier, n_req * heads)

    span_dst = raw.at[pl.ds(pl.multiple_of(prefix + me_ctx * tokens, tokens), tokens), both]
    pltpu.make_async_copy(span_send.at[col], span_dst, span_recv).start()

    def send_span(o, _):
        c = lax.rem(col + o, heads)
        pltpu.make_async_remote_copy(
            span_send.at[c], span_dst, span_sent, span_recv,
            device_id=(me_req, half * heads + c), device_id_type=MESH,
        ).start()
        return 0

    lax.fori_loop(1, heads, send_span, 0)

    page_dst = raw.at[pl.ds(pl.multiple_of((me_ctx * n_req + me_req) * page_len, page_len), page_len), both]
    pltpu.make_async_copy(send.at[me_req, col], page_dst, page_recv.at[col]).start()

    def send_page(req, c):
        pltpu.make_async_remote_copy(
            send.at[req, c], page_dst, page_sent, page_recv.at[col],
            device_id=(req, half * heads + c), device_id_type=MESH,
        ).start()

    def send_same(o, _):
        send_page(lax.rem(me_req + o, n_req), col)
        return 0

    lax.fori_loop(1, n_req, send_same, 0)

    def send_sides(o, _):
        req = lax.rem(me_req + o, n_req)
        send_page(req, lax.rem(col + 1, heads))
        send_page(req, lax.rem(col + heads - 1, heads))
        return 0

    lax.fori_loop(0, n_req, send_sides, 0)

    def send_far(o, _):
        send_page(lax.rem(me_req + o, n_req), lax.rem(col + 2, heads))
        return 0

    lax.fori_loop(0, n_req, send_far, 0)

    def unit_of(i):
        far = lax.div(i, 4)
        slot = (1 - far) * (1 + 2 * lax.rem(i, 2)) + far * 2
        return slot, (1 - far) * lax.div(i, 2) + far * (i - 4)

    def send_q(i, _):
        slot, h = unit_of(i)
        c = lax.rem(col + slot, heads)
        u = slot * 2 + h
        pltpu.make_async_remote_copy(
            q_src(c, h), qbuf.at[u], q_sent, q_recv.at[u],
            device_id=(me_req, half * heads + c), device_id_type=MESH,
        ).start()
        return 0

    units = 2 * (heads - 1)
    lax.fori_loop(0, units, send_q, 0)

    def settle(start, size, key0):
        at = pl.ds(start, size)
        keys = raw[at, 0:hd].astype(F32)
        dead = keys > 100.0
        kv[at, 0:hd] = jnp.where(dead, key0, keys).astype(BF16)
        kv[at, hd : 2 * hd] = raw[at, hd : 2 * hd]
        kv[at, 2 * hd :] = jnp.where(dead, 0.0, 1.0).astype(BF16)

    part_rows = part * group
    tiles = part_rows // ROWS
    toks = ROWS // group

    def attend(u, count, segments, fresh, last, first_token):
        base = u * part_rows
        steps = [(t, g) for t in range(count * tiles) for g in range(len(segments))]

        def score(t, g):
            start, size, _ = segments[g]
            q = qbuf[u + t // tiles, (t % tiles) * toks : (t % tiles + 1) * toks].reshape(ROWS, hd)
            return lax.dot_general(q, kv[pl.ds(start, size), 0:hd], NT, preferred_element_type=F32)

        following = score(*steps[0])
        for n, (t, g) in enumerate(steps):
            s = following * scale
            if n + 1 < len(steps):
                following = score(*steps[n + 1])
            start, size, first_key = segments[g]
            at = pl.ds(pl.multiple_of(base + t * ROWS, ROWS), ROWS)
            if first_key is not None:
                token = lax.broadcasted_iota(jnp.int32, (ROWS, size), 0) // group + (first_token + t * toks - first_key)
                key = lax.broadcasted_iota(jnp.int32, (ROWS, size), 1)
                s = jnp.where(key <= token, s, -1e30)
            top = jnp.max(s, axis=1, keepdims=True)
            if g == 0 and fresh:
                now = jnp.broadcast_to(top, (ROWS, hd))
            else:
                before = peak[at, :] if g == 0 else now
                now = jnp.maximum(before, top)
                factor = jnp.exp2(before - now)
            w = jnp.exp2(s - jnp.concatenate([now] * (size // hd), axis=1)).astype(BF16)
            wv = lax.dot_general(w, kv[pl.ds(start, size), hd:], NN, preferred_element_type=F32)
            if g == 0 and fresh:
                total = wv
            else:
                total = (acc[at, :] if g == 0 else total) * jnp.concatenate([factor, factor], axis=1) + wv
            if g + 1 == len(segments):
                if last:
                    out = total[:, 0:hd] / total[:, hd:]
                    ostage[u + t // tiles, (t % tiles) * toks : (t % tiles + 1) * toks] = out.astype(BF16).reshape(
                        toks, group, hd
                    )
                else:
                    peak[at, :] = now
                    acc[at, :] = total

    span_at = pl.multiple_of(prefix + half * span, span)
    whole(raw.at[pl.ds(span_at, span), both], span_recv).wait()
    span_pass = pltpu.make_async_remote_copy(
        raw.at[pl.ds(prefix, span), both], raw.at[pl.ds(prefix, span), both], span_pass_sent, span_pass_recv,
        device_id=partner, device_id_type=MESH,
    )

    @pl.when(half == 0)
    def _():
        span_pass.start()

    key0 = raw[pl.ds(span_at, 16), 0:hd].astype(F32)[0:1, :]
    settle(span_at, span, key0)
    own_rows = slice(0, 2 * part_rows)
    acc[own_rows, :] = jnp.zeros((2 * part_rows, 2 * hd), F32)
    peak[own_rows, :] = jnp.full((2 * part_rows, hd), -1e30, F32)
    for h in range(2):
        whole(qbuf.at[h], q_recv.at[h]).wait()

    def chunk(i, _):
        c = lax.rem(col + (1 - lax.div(i, 3)) * i * (heads - 1) * (1 - lax.div(i, 2)) + lax.div(i, 2) * (i - 1), heads)
        start = pl.multiple_of((half * heads + c) * per_slot, per_slot)
        here = raw.at[pl.ds(start, per_slot), both]
        whole(here, page_recv.at[c]).wait()
        pltpu.make_async_remote_copy(
            here, here, pass_sent, pass_recv.at[c], device_id=partner, device_id_type=MESH
        ).start()
        settle(start, per_slot, key0)
        attend(0, 2, [(start, per_slot, None)], False, False, None)
        return 0

    lax.fori_loop(0, heads, chunk, 0)
    near_at = pl.multiple_of(half * near, near)
    far_at = pl.multiple_of((1 - half) * near, near)
    cut = near // 2

    def halves_of(at):
        return [(pl.multiple_of(at + i * cut, cut), cut, None) for i in range(2)]

    def first_pass(i, _):
        slot, h = unit_of(i)
        u = slot * 2 + h
        whole(qbuf.at[u], q_recv.at[u]).wait()
        attend(u, 1, halves_of(near_at), True, False, None)
        return 0

    lax.fori_loop(0, units, first_pass, 0)

    for c in range(heads):
        start = pl.multiple_of(far_at + c * per_slot, per_slot)
        whole(raw.at[pl.ds(start, per_slot), both], pass_recv.at[c]).wait()
        settle(start, per_slot, key0)

    @pl.when(half == 1)
    def _():
        span_pass.wait_recv()
        settle(prefix, span, key0)

    def second_pass(j, _):
        own = lax.div(j, units)
        slot, h = unit_of((1 - own) * (units - 1 - j))
        slot = (1 - own) * slot
        h = (1 - own) * h + own * (j - units)
        u = slot * 2 + h
        from_col = lax.rem(col - slot + heads, heads)
        first_token = from_col * tokens + h * part
        for z in range(halves):

            @pl.when(half == z)
            def _():
                spans = [(prefix + i * span, span, 0 if i == z else None) for i in range(z + 1)]
                attend(u, 1, halves_of(far_at) + spans, False, True, first_token)

        o_dst = out_hbm.at[pl.ds(pl.multiple_of(h * part, part), part), pl.ds(pl.multiple_of(col * group, group), group), :]

        @pl.when(own == 1)
        def _():
            pltpu.make_async_copy(ostage.at[u], o_dst, own_sem).start()

        @pl.when(own == 0)
        def _():
            pltpu.make_async_remote_copy(
                ostage.at[u], o_dst, o_sent, o_recv,
                device_id=(me_req, half * heads + from_col), device_id_type=MESH,
            ).start()

        return 0

    lax.fori_loop(0, 2 * heads, second_pass, 0)
    whole(ostage.at[pl.ds(0, 2)], own_sem).wait()
    whole(raw.at[pl.ds(0, (heads - 1) * tokens), both], span_sent).wait()
    whole(raw.at[pl.ds(0, (n_req * heads - 1) * page_len), both], page_sent).wait()
    whole(raw.at[pl.ds(0, near), both], pass_sent).wait()

    @pl.when(half == 0)
    def _():
        span_pass.wait_send()

    whole(qbuf.at[pl.ds(0, units)], q_sent).wait()
    whole(ostage.at[pl.ds(0, units)], o_sent).wait()
    whole(ostage.at[pl.ds(0, units)], o_recv).wait()


def per_device(queries, span_keys, span_values, store_keys, store_values, page_home, hits, counts):
    n_req = lax.axis_size("req")
    n_ctx = lax.axis_size("ctx")
    _, tokens, q_heads, hd = queries.shape
    heads = span_keys.shape[2]
    group = q_heads // heads
    _, store_dev, page_len, _, _ = store_keys.shape
    dims = (n_req, n_ctx, heads, store_dev, page_len, tokens, group, hd)
    rows = heads * tokens * group
    keys = n_req * n_ctx * page_len + n_ctx * tokens
    smem = pl.BlockSpec(memory_space=pltpu.SMEM)
    hbm = pl.BlockSpec(memory_space=pl.ANY)
    dma = pltpu.SemaphoreType.DMA
    out = pl.pallas_call(
        functools.partial(kernel, dims),
        out_shape=jax.ShapeDtypeStruct((tokens, q_heads, hd), BF16),
        in_specs=[smem] * 3 + [hbm] * 5,
        out_specs=hbm,
        scratch_shapes=[
            pltpu.VMEM((2, store_dev, page_len * heads, hd), BF16),
            pltpu.VMEM((2, tokens * heads, hd), BF16),
            pltpu.VMEM((n_req, heads, page_len, 2 * hd), BF16),
            pltpu.VMEM((heads, tokens, 2 * hd), BF16),
            pltpu.VMEM((2 * heads, tokens // 2, group, hd), BF16),
            pltpu.VMEM((keys, 2 * hd), BF16),
            pltpu.VMEM((keys, 3 * hd), BF16),
            pltpu.VMEM((rows, 2 * hd), F32),
            pltpu.VMEM((rows, hd), F32),
            pltpu.VMEM((2 * heads, tokens // 2, group, hd), BF16),
            dma((4,)),
            dma, dma((heads,)), dma, dma, dma, dma((heads,)), dma, dma, dma, dma((2 * heads,)), dma, dma, dma,
        ],
        compiler_params=pltpu.CompilerParams(
            collective_id=0, has_side_effects=True, vmem_limit_bytes=60 * 2**20
        ),
        name="attend_pages",
    )(
        hits, counts, page_home, queries[0],
        span_keys.reshape(tokens * heads, hd),
        span_values.reshape(tokens * heads, hd),
        store_keys.reshape(store_dev, page_len * heads, hd),
        store_values.reshape(store_dev, page_len * heads, hd),
    )
    return out[None]


def solution(mesh):
    placed = (
        P("req", "ctx", None, None),
        P("req", "ctx", None, None),
        P("req", "ctx", None, None),
        P("ctx", "req", None, None, None),
        P("ctx", "req", None, None, None),
        P("ctx", None),
        P(),
        P(),
    )
    return jax.shard_map(
        per_device,
        mesh=mesh,
        in_specs=placed,
        out_specs=P("req", "ctx", None, None),
        check_vma=False,
    )
```

time: 422 us -> 89.3 us (0.21); the launches traced: 415 us -> 88.8 us
  matrix products: 193 us -> 0 us
  other arithmetic: 110 us -> 0 us
  Pallas kernels: 0 us -> 85.7 us
  waiting for transfers between devices: 67.6 us -> 0 us
  local copies, waits for them, and re-layouts: 20.5 us -> 3.08 us
  between operations: 14 us -> 0.01 us
  starting transfers between devices: 9.82 us -> 0 us
    dot_general x20 -> x0, matrix products: 193 us -> none  [the longest x10 115 us: attend(): jnp.einsum('tkgs,skd->tkgd', weights.astype(jnp.bfloat16), values, prefer...]
    reduce_sum x13 -> x0, other arithmetic: 96.2 us -> none  [the longest x10 94.5 us: attend(): total = total * factor + jnp.sum(weights, axis=-1)]
    pallas_call x0 -> x1, Pallas kernels: none -> 85.7 us  [per_device(): pl.pallas_call(functools.partial(kernel, dims), out_shape=jax.ShapeDtypeS...]
    all_gather x2 -> x0, waiting for transfers between devices: 57.8 us -> none  [the longest x1 57.7 us: per_device(): lax.all_gather(block_keys, 'ctx', axis=0, tiled=True)]
    all_to_all x2 -> x0, waiting for transfers between devices: 9.85 us -> none  [the longest x1 9.85 us: per_device(): lax.all_to_all(send_keys, 'req', split_axis=0, concat_axis=0, tiled=True)]
    all_to_all x2 -> x0, starting transfers between devices: 9.22 us -> none  [the longest x1 5.63 us: per_device(): lax.all_to_all(send_keys, 'req', split_axis=0, concat_axis=0, tiled=True)]
    gather x6 -> x0, local copies, waits for them, and re-layouts: 6.24 us -> none  [the longest x1 2.65 us: per_device(): store_keys[0][local_slot]]
    select_n x6 -> x0, other arithmetic: 5.99 us -> none  [the longest x2 3.65 us: per_device(): jnp.where(is_prefix[None, :], page_live[None, :], key_pos[None, :] <= que...]
  transfers between devices with their start and end apart: 4 -> 0, of which waited for: 2 -> 0; matrix products, arithmetic and copies ran while one was open for 45% -> 0% of each run, Pallas kernels for 0% -> 0%
where the time goes in v2:
time: 89.3 us; the launch traced here: 88.8 us
  Pallas kernels  85.7 us (96%)
  local copies, waits for them, and re-layouts  3.08 us (3%)
    pallas_call x1, Pallas kernels, per_device(): pl.pallas_call(functools.partial(kernel, dims), out_shape=jax.ShapeDtypeS...  85.7 us
    unnamed x1, local copies, waits for them, and re-layouts  3.08 us

profile of v2, /device:TPU:64, one launch (start us, length us, event | category | flops | bytes accessed | tf_op | source)
XLA Modules:
  0.0 88.8 jit_solution(12406455259661183279)
XLA Ops:
  0.0 85.7 %attend_pages.1 = bf16[128,64,128]{2,1,0:T(8,128)(2,1)} custom-call(s32[16,128]{1,0:T(8,128)} %hits.1, s32[16]{0:T(128)} %counts.1, s32[1,512]{1,0:T(1,128)} %home.1, bf16[128,64,128]{2,1,0:T(8,128)(2,1)} %bitcast.7, bf16[512,128]{1,0:T(8,128)(2,1)} %bitcast.10, bf16[512,128]{1,0:T(8,128)(2,1)} %bitcast.11, bf16[32,128,128]{2,1,0:T(8,128)(2,1)} %bitcast.8, ...), custom_call_target="tpu_custom_call" | custom-call | tf_op jit(solution)/shard_map/attend_pages/pallas_call | solution.py:342
  85.7 3.1 %copy.10 = bf16[1,128,64,128]{3,2,1,0:T(8,128)(2,1)} copy(bf16[1,128,64,128]{3,2,1,0:T(8,128)(2,1)} %bitcast.6) | data formatting | bytes 4194304

commit v3 on v2

--- a/solution.py
+++ b/solution.py
@@ -86,14 +86,17 @@
     for load in loads[2:]:
         load.wait()
 
-    def pack(r, _):
+    first_row = me_req * store_dev
+    group_of = 4
+
+    def pack(r):
         slot = jnp.int32(0)
         live = jnp.int32(0)
         for i in range(n_req):
             j = i * n_ctx + me_ctx
-            row = home[0, hits[r, j]]
-            mine = (lax.div(row, store_dev) == me_req).astype(jnp.int32)
-            slot = slot + mine * lax.rem(row, store_dev)
+            row = home[0, hits[r, j]] - first_row
+            mine = jnp.logical_and(row >= 0, row < store_dev).astype(jnp.int32)
+            slot = slot + mine * row
             live = live + mine * (j < counts[r]).astype(jnp.int32)
         live = live.astype(F32)
         pair = jnp.concatenate([store[0, slot], store[1, slot]], axis=1)
@@ -103,9 +106,13 @@
         moved = (moved * live + filler * (1.0 - live)).astype(BF16)
         for h in range(heads):
             send[r, h] = moved[h * page_len : (h + 1) * page_len, :]
-        return 0
-
-    lax.fori_loop(0, n_req, pack, 0)
+
+    def pack_group(i, _):
+        for k in range(group_of):
+            pack(i * group_of + k)
+        return 0
+
+    lax.fori_loop(0, n_req // group_of, pack_group, 0)
     pl.semaphore_wait(barrier, n_req * heads)
 
     span_dst = raw.at[pl.ds(pl.multiple_of(prefix + me_ctx * tokens, tokens), tokens), both]
@@ -130,14 +137,17 @@
             device_id=(req, half * heads + c), device_id_type=MESH,
         ).start()
 
+    def mixed(o):
+        return lax.rem(me_req + 5 * o, n_req)
+
     def send_same(o, _):
-        send_page(lax.rem(me_req + o, n_req), col)
+        send_page(mixed(o), col)
         return 0
 
     lax.fori_loop(1, n_req, send_same, 0)
 
     def send_sides(o, _):
-        req = lax.rem(me_req + o, n_req)
+        req = mixed(o)
         send_page(req, lax.rem(col + 1, heads))
         send_page(req, lax.rem(col + heads - 1, heads))
         return 0
@@ -145,7 +155,7 @@
     lax.fori_loop(0, n_req, send_sides, 0)
 
     def send_far(o, _):
-        send_page(lax.rem(me_req + o, n_req), lax.rem(col + 2, heads))
+        send_page(mixed(o), lax.rem(col + 2, heads))
         return 0
 
     lax.fori_loop(0, n_req, send_far, 0)
@@ -293,8 +303,13 @@
 
             @pl.when(half == z)
             def _():
-                spans = [(prefix + i * span, span, 0 if i == z else None) for i in range(z + 1)]
-                attend(u, 1, halves_of(far_at) + spans, False, True, first_token)
+                spans = [(prefix + i * span, span, None) for i in range(z)]
+                for w in range(2):
+
+                    @pl.when(lax.div(from_col, heads // 2) == w)
+                    def _():
+                        last_keys = (prefix + z * span, (w + 1) * span // 2, 0)
+                        attend(u, 1, halves_of(far_at) + spans + [last_keys], False, True, first_token)
 
         o_dst = out_hbm.at[pl.ds(pl.multiple_of(h * part, part), part), pl.ds(pl.multiple_of(col * group, group), group), :]
 

time: 89.3 us -> 86.9 us (0.973)
  Pallas kernels: 85.7 us -> 83.6 us
    pallas_call x1, Pallas kernels: 85.7 us -> 83.6 us  [per_device(): pl.pallas_call(functools.partial(kernel, dims), out_shape=jax.ShapeDtypeS...]
where the time goes in v3:
time: 86.9 us; the launch traced here: 86.7 us
  Pallas kernels  83.6 us (96%)
  local copies, waits for them, and re-layouts  3.08 us (4%)
    pallas_call x1, Pallas kernels, per_device(): pl.pallas_call(functools.partial(kernel, dims), out_shape=jax.ShapeDtypeS...  83.6 us
    unnamed x1, local copies, waits for them, and re-layouts  3.08 us

profile of v3, /device:TPU:64, one launch (start us, length us, event | category | flops | bytes accessed | tf_op | source)
XLA Modules:
  0.0 86.7 jit_solution(17751968632138880945)
XLA Ops:
  0.0 83.6 %attend_pages.1 = bf16[128,64,128]{2,1,0:T(8,128)(2,1)} custom-call(s32[16,128]{1,0:T(8,128)} %hits.1, s32[16]{0:T(128)} %counts.1, s32[1,512]{1,0:T(1,128)} %home.1, bf16[128,64,128]{2,1,0:T(8,128)(2,1)} %bitcast.7, bf16[512,128]{1,0:T(8,128)(2,1)} %bitcast.10, bf16[512,128]{1,0:T(8,128)(2,1)} %bitcast.11, bf16[32,128,128]{2,1,0:T(8,128)(2,1)} %bitcast.8, ...), custom_call_target="tpu_custom_call" | custom-call | tf_op jit(solution)/shard_map/attend_pages/pallas_call | solution.py:357
  83.6 3.1 %copy.10 = bf16[1,128,64,128]{3,2,1,0:T(8,128)(2,1)} copy(bf16[1,128,64,128]{3,2,1,0:T(8,128)(2,1)} %bitcast.6) | data formatting | bytes 4194304

commit v4 on v3

--- a/solution.py
+++ b/solution.py
@@ -384,6 +384,30 @@
         store_keys.reshape(store_dev, page_len * heads, hd),
         store_values.reshape(store_dev, page_len * heads, hd),
     )
+    pieces = 4
+
+    def hand_over(src, dst, held, arrived, left):
+        size = tokens // pieces
+        at = [pl.ds(i * size, size) for i in range(pieces)]
+        gets = [pltpu.make_async_copy(src.at[at[i]], held.at[at[i]], arrived.at[i]) for i in range(pieces)]
+        puts = [pltpu.make_async_copy(held.at[at[i]], dst.at[at[i]], left.at[i]) for i in range(pieces)]
+        for get in gets:
+            get.start()
+        for get, put in zip(gets, puts):
+            get.wait()
+            put.start()
+        for put in puts:
+            put.wait()
+
+    out = pl.pallas_call(
+        hand_over,
+        out_shape=jax.ShapeDtypeStruct(out.shape, out.dtype),
+        in_specs=[hbm],
+        out_specs=hbm,
+        scratch_shapes=[pltpu.VMEM(out.shape, out.dtype), dma((pieces,)), dma((pieces,))],
+        compiler_params=pltpu.CompilerParams(vmem_limit_bytes=60 * 2**20),
+        name="hand_over",
+    )(out)
     return out[None]
 
 

time: 86.9 us -> 86.4 us (level)
  local copies, waits for them, and re-layouts: 3.08 us -> 0 us
  Pallas kernels: 83.6 us -> 86 us
    unnamed x1 -> x0, local copies, waits for them, and re-layouts: 3.08 us -> none
    pallas_call x0 -> x1, Pallas kernels: none -> 2.42 us  [per_device(): pl.pallas_call(hand_over, out_shape=jax.ShapeDtypeStruct(out.shape, out.d...]
where the time goes in v4:
time: 86.4 us; the launch traced here: 86.2 us
  Pallas kernels  86 us (100%)
    pallas_call x1, Pallas kernels, per_device(): pl.pallas_call(functools.partial(kernel, dims), out_shape=jax.ShapeDtypeS...  83.6 us
    pallas_call x1, Pallas kernels, per_device(): pl.pallas_call(hand_over, out_shape=jax.ShapeDtypeStruct(out.shape, out.d...  2.42 us

profile of v4, /device:TPU:64, one launch (start us, length us, event | category | flops | bytes accessed | tf_op | source)
XLA Modules:
  0.0 86.2 jit_solution(3691482916390927226)
XLA Ops:
  0.0 83.6 %attend_pages.1.src = bf16[128,64,128]{2,1,0:T(8,128)(2,1)} custom-call(s32[16,128]{1,0:T(8,128)} %hits.1, s32[16]{0:T(128)} %counts.1, s32[1,512]{1,0:T(1,128)} %home.1, bf16[128,64,128]{2,1,0:T(8,128)(2,1)} %bitcast.6, bf16[512,128]{1,0:T(8,128)(2,1)} %bitcast.9, bf16[512,128]{1,0:T(8,128)(2,1)} %bitcast.10, bf16[32,128,128]{2,1,0:T(8,128)(2,1)} %bitcast.7, ...), custom_call_target="tpu_custom_call" | custom-call | tf_op jit(solution)/shard_map/attend_pages/pallas_call | solution.py:357
  83.6 2.4 %hand_over.1 = bf16[128,64,128]{2,1,0:T(8,128)(2,1)} custom-call(bf16[128,64,128]{2,1,0:T(8,128)(2,1)} %attend_pages.1.src), custom_call_target="tpu_custom_call" | custom-call | tf_op jit(solution)/shard_map/hand_over/pallas_call | solution.py:402
